TPU v7x, 32 devices: a whole 2x2x4 slice. The times are simulated.
32 devices in a mesh: grp: 2 (over y), blk: 4 (over z), uly: 4 (over x, core).
Axes of the slice: x: 2, y: 2, z: 4, core: 2. Of those that a mesh axis runs over, the one named last changes fastest.
Arguments:
- queries: bfloat16 [16384, 1024], P(('grp', 'blk', 'uly')), parts along dimension 0, may hold values from -6 to 6
- keys: bfloat16 [16384, 1024], P(('grp', 'blk', 'uly')), parts along dimension 0, may hold values from -6 to 6
- values: bfloat16 [16384, 1024], P(('grp', 'blk', 'uly')), parts along dimension 0, may hold values from -6 to 6
- grad_out: bfloat16 [16384, 1024], P(('grp', 'blk', 'uly')), parts along dimension 0, may hold values from -256 to 256
- key_lists: int32 [128, 12], P('grp'), parts along dimension 0, may hold values from 0 to 63, as said below
- list_length: int32 [128], P('grp'), parts along dimension 0, may hold values from 1 to 12, as said below
Outputs:
- grad_queries: bfloat16 [16384, 1024], P(('grp', 'blk', 'uly')), parts along dimension 0
- grad_keys: bfloat16 [16384, 1024], P(('grp', 'blk', 'uly')), parts along dimension 0
- grad_values: bfloat16 [16384, 1024], P(('grp', 'blk', 'uly')), parts along dimension 0
There are 2 independent parts, one for each index of `grp`. A program takes and returns all parts, laid end to end along the dimension named above; each array names one. Nothing has to cross between parts.
Inputs may be any that keep to these rules, and one draw needn't show every extreme that they name: `key_lists`: row i lists 12 different key-block numbers, each within 6 blocks of i counting around the slab's end, its own block i first; only its first list_length[i] entries count. `list_length`: some query block lists exactly 12 key blocks.
All inputs are finite; a program needn't handle non-finite values.
Results may differ from a plain program's by a relative error of at most 0.0087.
Values may be sent and summed in bfloat16 or wider, within the bound.
A program may use at most 128 MiB of HBM per device.

v0:
```python
import functools

import jax
import jax.numpy as jnp
from jax import lax
from jax.experimental import pallas as pl
from jax.experimental.pallas import tpu as pltpu
from jax.sharding import PartitionSpec as P

HD = 64
BS = 128
REACHB = 6
PAIR = 2 * HD
SCALE = HD ** (-0.5)
NT = (((1,), (1,)), ((), ()))
MIB = 1024 * 1024


def block_diagonal(pair, factor):
    wide = pair.astype(jnp.float32) * factor
    lane = lax.broadcasted_iota(jnp.int32, wide.shape, 1)
    first = jnp.where(lane < HD, wide, 0.0).astype(jnp.bfloat16)
    second = jnp.where(lane < HD, 0.0, wide).astype(jnp.bfloat16)
    return first, second


def attend_kernel(
    spots_ref, lengths_ref, q_ref, do_ref, kl_ref, ko_ref, kr_ref, vl_ref, vo_ref, vr_ref,
    dq_ref, own_ref, left_ref, right_ref,
    k_scr, v_scr, kt_scr, acc_k, acc_v, s_scr, p_scr, q_bd, do_bd, dqt_scr, round_scr, sems,
):
    step = pl.program_id(0)
    steps = pl.num_programs(0)
    halo, feat = kl_ref.shape
    rows = ko_ref.shape[0]
    total = k_scr.shape[0]
    packs = feat // PAIR

    @pl.when(step == 0)
    def _():
        copies = []
        for dst, parts in ((k_scr, (kl_ref, ko_ref, kr_ref)), (v_scr, (vl_ref, vo_ref, vr_ref))):
            start = 0
            for part in parts:
                size = part.shape[0]
                copies.append(
                    pltpu.make_async_copy(part, dst.at[pl.ds(start, size)], sems.at[len(copies)])
                )
                start += size
        for copy in copies:
            copy.start()

        @pl.loop(0, total // BS)
        def _(b):
            at = pl.ds(b * BS, BS)
            acc_k[at, :] = jnp.zeros((BS, feat), jnp.float32)
            acc_v[at, :] = jnp.zeros((BS, feat), jnp.float32)

        for copy in copies:
            copy.wait()

        @pl.loop(0, total // BS)
        def _(b):
            kt_scr[pl.ds(b * feat, feat), :] = k_scr[pl.ds(b * BS, BS), :].T

    for g in range(packs):
        cols = slice(g * PAIR, (g + 1) * PAIR)
        first, second = block_diagonal(q_ref[:, cols], SCALE)
        q_bd[g, :BS, :] = first
        q_bd[g, BS:, :] = second
        first, second = block_diagonal(do_ref[:, cols], 1.0)
        do_bd[g, :BS, :] = first
        do_bd[g, BS:, :] = second

    length = lengths_ref[step]

    def scores(slot, carry):
        at = pl.ds(pl.multiple_of(spots_ref[step, slot] * BS, BS), BS)
        out = []
        for g in range(packs):
            top, sums, cross = carry[g]
            cols = slice(g * PAIR, (g + 1) * PAIR)
            s = lax.dot_general(k_scr[at, cols], q_bd[g], NT, preferred_element_type=jnp.float32)
            dp = lax.dot_general(v_scr[at, cols], do_bd[g], NT, preferred_element_type=jnp.float32)
            s_scr[slot, g] = s
            p_scr[slot, g] = dp
            s = s.reshape(BS // 8, 8, 2 * BS)
            dp = dp.reshape(BS // 8, 8, 2 * BS)
            new_top = jnp.maximum(top, jnp.max(s, axis=0))
            keep = jnp.exp(top - new_top)
            p = jnp.exp(s - new_top[None])
            out.append(
                (
                    new_top,
                    sums * keep + jnp.sum(p, axis=0),
                    cross * keep + jnp.sum(p * dp, axis=0),
                )
            )
        return tuple(out)

    blank = jnp.zeros((8, 2 * BS), jnp.float32)
    start = tuple((blank - jnp.inf, blank, blank) for _ in range(packs))
    stats = lax.fori_loop(0, length, scores, start)
    merged = []
    for top, sums, cross in stats:
        best = jnp.max(top, axis=0, keepdims=True)
        factor = jnp.exp(top - best)
        denom = jnp.sum(sums * factor, axis=0, keepdims=True)
        delta = jnp.sum(cross * factor, axis=0, keepdims=True) / denom
        merged.append((best + jnp.log(denom), delta))

    dqt_scr[...] = jnp.zeros_like(dqt_scr)

    @pl.loop(0, length)
    def _(slot):
        spot = spots_ref[step, slot]
        at = pl.ds(pl.multiple_of(spot * BS, BS), BS)
        for g in range(packs):
            log_total, delta = merged[g]
            cols = slice(g * PAIR, (g + 1) * PAIR)
            weight = jnp.exp(s_scr[slot, g] - log_total)
            grad = (weight * (p_scr[slot, g] - delta)).astype(jnp.bfloat16)
            half = weight.astype(jnp.bfloat16)
            acc_v[at, cols] += jnp.dot(half, do_bd[g], preferred_element_type=jnp.float32)
            acc_k[at, cols] += jnp.dot(grad, q_bd[g], preferred_element_type=jnp.float32)
            for h in range(2):
                low = g * PAIR + h * HD
                kt = kt_scr[pl.ds(pl.multiple_of(spot * feat + low, HD), HD), :]
                dqt_scr[low : low + HD, :] += jnp.dot(
                    kt, grad[:, h * BS : (h + 1) * BS], preferred_element_type=jnp.float32
                )

    dq_ref[...] = (dqt_scr[...].T * SCALE).astype(jnp.bfloat16)

    @pl.when(step == steps - 1)
    def _():
        @pl.loop(0, total // BS)
        def _(b):
            at = pl.ds(b * BS, BS)
            round_scr[0, at, :] = acc_k[at, :].astype(jnp.bfloat16)
            round_scr[1, at, :] = acc_v[at, :].astype(jnp.bfloat16)

        copies = []
        for i, acc in enumerate((acc_k, acc_v)):
            copies += [
                pltpu.make_async_copy(acc.at[pl.ds(halo, rows)], own_ref.at[i], sems.at[3 * i]),
                pltpu.make_async_copy(
                    round_scr.at[i, pl.ds(0, halo)], left_ref.at[i], sems.at[3 * i + 1]
                ),
                pltpu.make_async_copy(
                    round_scr.at[i, pl.ds(halo + rows, halo)], right_ref.at[i], sems.at[3 * i + 2]
                ),
            ]
        for copy in copies:
            copy.start()
        for copy in copies:
            copy.wait()


def attend(spots, lengths, q, do, k_parts, v_parts):
    rows, feat = q.shape
    halo = k_parts[0].shape[0]
    total = rows + 2 * halo
    packs = feat // PAIR
    slots = spots.shape[1]
    hbm = pl.BlockSpec(memory_space=pl.ANY)
    block = pl.BlockSpec((BS, feat), lambda i, *_: (i, 0))
    f32, bf16 = jnp.float32, jnp.bfloat16
    return pl.pallas_call(
        attend_kernel,
        grid_spec=pltpu.PrefetchScalarGridSpec(
            num_scalar_prefetch=2,
            grid=(rows // BS,),
            in_specs=[block, block] + [hbm] * 6,
            out_specs=[block, hbm, hbm, hbm],
            scratch_shapes=[
                pltpu.VMEM((total, feat), bf16),
                pltpu.VMEM((total, feat), bf16),
                pltpu.VMEM((total // BS * feat, BS), bf16),
                pltpu.VMEM((total, feat), f32),
                pltpu.VMEM((total, feat), f32),
                pltpu.VMEM((slots, packs, BS, 2 * BS), f32),
                pltpu.VMEM((slots, packs, BS, 2 * BS), f32),
                pltpu.VMEM((packs, 2 * BS, PAIR), bf16),
                pltpu.VMEM((packs, 2 * BS, PAIR), bf16),
                pltpu.VMEM((feat, BS), f32),
                pltpu.VMEM((2, total, feat), bf16),
                pltpu.SemaphoreType.DMA((6,)),
            ],
        ),
        out_shape=[
            jax.ShapeDtypeStruct((rows, feat), bf16),
            jax.ShapeDtypeStruct((2, rows, feat), f32),
            jax.ShapeDtypeStruct((2, halo, feat), bf16),
            jax.ShapeDtypeStruct((2, halo, feat), bf16),
        ],
        compiler_params=pltpu.CompilerParams(vmem_limit_bytes=48 * MIB),
        name="attend",
    )(spots, lengths, q, do, *k_parts, *v_parts)


def passed_along(block, axis, distance):
    count = lax.axis_size(axis)
    return lax.ppermute(block, axis, [((i - distance) % count, i) for i in range(count)])


def local_lists(key_lists, list_length, per_rank):
    block_rank = lax.axis_index("blk")
    all_blocks = per_rank * lax.axis_size("blk")
    base_block = block_rank * per_rank - REACHB
    lists_here = lax.dynamic_slice_in_dim(key_lists, block_rank * per_rank, per_rank, 0)
    lengths_here = lax.dynamic_slice_in_dim(list_length, block_rank * per_rank, per_rank, 0)
    return (lists_here - base_block) % all_blocks, lengths_here


def shards(queries, keys, values, grad_out, key_lists, list_length):
    stacked = jnp.stack([queries, keys, values, grad_out])
    spread = lax.all_to_all(stacked, "uly", split_axis=2, concat_axis=1, tiled=True)
    q, k, v, do = spread[0], spread[1], spread[2], spread[3]
    rows = q.shape[0]
    halo = REACHB * BS
    spots, lengths = local_lists(key_lists, list_length, rows // BS)
    pair = jnp.stack([k, v])
    from_left = passed_along(pair[:, rows - halo :], "blk", 1)
    from_right = passed_along(pair[:, :halo], "blk", -1)
    dq, own, left, right = attend(
        spots, lengths, q, do,
        (from_left[0], k, from_right[0]), (from_left[1], v, from_right[1]),
    )
    from_right = passed_along(left, "blk", -1).astype(jnp.float32)
    from_left = passed_along(right, "blk", 1).astype(jnp.float32)
    own = own.at[:, rows - halo :].add(from_right)
    own = own.at[:, :halo].add(from_left)
    result = jnp.concatenate([dq[None], own.astype(jnp.bfloat16)])
    returned = lax.all_to_all(result, "uly", split_axis=1, concat_axis=2, tiled=True)
    return (returned[0], returned[1], returned[2])


def solution(mesh):
    rows = P(("grp", "blk", "uly"), None)
    return jax.shard_map(
        shards,
        mesh=mesh,
        in_specs=(rows, rows, rows, rows, P("grp", None), P("grp")),
        out_specs=(rows, rows, rows),
        check_vma=False,
    )
```

profile of v0, /device:TPU:1, one launch (start us, length us, event | category | flops | bytes accessed | tf_op | source)
XLA Modules:
  0.0 315.5 jit_solution(12377456334912981741)
XLA Ops:
  0.6 0.0 copy-start
  0.6 3.8 %pad_maximum_fusion = bf16[4,512,1024]{2,1,0:T(8,128)(2,1)} fusion(bf16[1,512,1024]{2,1,0:T(8,128)(2,1)} %bitcast.49, bf16[1,512,1024]{2,1,0:T(8,128)(2,1)} %bitcast.50, bf16[1,512,1024]{2,1,0:T(8,128)(2,1)} %bitcast.51, bf16[1,512,1024]{2,1,0:T(8,128)(2,1)} %bitcast.52), kind=kLoop, calls=%fused_computation | loop fusion | flops 6291456 | bytes 8388608 | tf_op jit(solution)/shard_map/stack | solution.py:217
  4.4 7.8 %copy.25 = bf16[4,512,1024]{1,0,2:T(4,128)(2,1)} copy(bf16[4,512,1024]{2,1,0:T(8,128)(2,1)} %pad_maximum_fusion) | data formatting | bytes 8388608 | tf_op jit(solution)/shard_map/stack | solution.py:217
  12.2 53.5 %all_to_all.30 = bf16[4,512,1024]{1,0,2:T(4,128)(2,1)} all-to-all(bf16[4,512,1024]{1,0,2:T(4,128)(2,1)} %copy.25), channel_id=1, replica_groups=mesh['grp'=2,'blk'=4,'uly'=4] {'uly'}, dimensions={2} | all-to-all | bytes 8388608 | tf_op jit(solution)/shard_map/all_to_all | solution.py:218
  65.7 7.4 %copy.26 = bf16[4,512,4,256]{3,1,2,0:T(8,128)(2,1)} copy(bf16[4,512,4,256]{1,0,3,2:T(4,128)(2,1)} %bitcast.37) | data formatting | bytes 8388608 | tf_op jit(solution)/shard_map/all_to_all | solution.py:218
  73.2 3.4 %fusion.3 = (bf16[1,4,512,256]{3,2,1,0:T(8,128)(2,1)S(1)}, bf16[1,4,512,256]{3,2,1,0:T(8,128)(2,1)S(1)}, bf16[1,4,512,256]{3,2,1,0:T(8,128)(2,1)}, bf16[1,4,512,256]{3,2,1,0:T(8,128)(2,1)S(1)}) fusion(bf16[4,4,512,256]{3,2,1,0:T(8,128)(2,1)} %bitcast.36), kind=kLoop, calls=%fused_computation.17 | loop fusion | bytes 8388608 | tf_op jit(solution)/shard_map/slice | solution.py:219
  76.6 0.0 copy-start.1
  76.6 0.0 copy-start.2
  76.6 0.0 copy-start.3
  76.6 1.4 pad_maximum_fusion.2
  78.0 4.1 %collective-permute-start.1 = (bf16[2,768,256]{2,1,0:T(8,128)(2,1)}, bf16[2,768,256]{2,1,0:T(8,128)(2,1)}, u32[]{:S(2)}, u32[]{:S(2)}) collective-permute-start(bf16[2,768,256]{2,1,0:T(8,128)(2,1)} %get-tuple-element.42), channel_id=1, source_target_pairs={{4,0},{8,4},{12,8},{0,12},{5,1},{9,5},{13,9},{1,13},{6,2},{10,6},{... | collective-permute-start | bytes 2359304 | tf_op jit(solution)/shard_map/ppermute | solution.py:204
  82.1 0.0 collective-permute-start
  82.1 0.0 copy-done.3
  82.1 0.1 dynamic_slice.7.lengths_ref
  82.2 0.0 copy-done
  82.2 0.1 constant_dynamic-slice_fusion
  82.3 0.1 copy.31
  82.4 15.9 %collective-permute-done.1 = bf16[2,768,256]{2,1,0:T(8,128)(2,1)} collective-permute-done((bf16[2,768,256]{2,1,0:T(8,128)(2,1)}, bf16[2,768,256]{2,1,0:T(8,128)(2,1)}, u32[]{:S(2)}, u32[]{:S(2)}) %collective-permute-start.1) | collective-permute-done | bytes 786464 | tf_op jit(solution)/shard_map/ppermute | solution.py:204
  98.3 1.2 slice_bitcast_fusion
  99.5 16.5 %collective-permute-done = bf16[2,768,256]{2,1,0:T(8,128)(2,1)} collective-permute-done((bf16[2,768,256]{2,1,0:T(8,128)(2,1)}, bf16[2,768,256]{2,1,0:T(8,128)(2,1)}, u32[]{:S(2)}, u32[]{:S(2)}) %collective-permute-start) | collective-permute-done | bytes 786464 | tf_op jit(solution)/shard_map/ppermute | solution.py:204
  116.0 1.2 slice_bitcast_fusion.1
  117.1 0.0 copy-done.1
  117.1 0.0 copy-done.2
  117.2 75.5 %attend.1 = (bf16[2048,256]{1,0:T(8,128)(2,1)S(1)}, f32[2,2048,256]{2,1,0:T(8,128)}, bf16[2,768,256]{2,1,0:T(8,128)(2,1)S(1)}, bf16[2,768,256]{2,1,0:T(8,128)(2,1)S(1)}) custom-call(s32[16,12]{1,0:T(8,128)S(1)} %add_select_fusion.spots_ref, s32[16]{0:T(128)S(1)} %dynamic_slice.7.lengths_ref, bf16[2048,256]{1,0:T(8,128)(2,1)S(1)} %bitcast.33, ...), custom_call_target="tpu_custom_call" | custom-call | tf_op jit(solution)/shard_map/attend/pallas_call | solution.py:169
  192.7 0.1 collective-permute-start.2
  192.8 1.5 collective-permute-start.3
  194.2 32.5 %collective-permute-done.2 = bf16[2,768,256]{2,1,0:T(8,128)(2,1)S(1)} collective-permute-done((bf16[2,768,256]{2,1,0:T(8,128)(2,1)S(1)}, bf16[2,768,256]{2,1,0:T(8,128)(2,1)S(1)}, u32[]{:S(2)}, u32[]{:S(2)}) %collective-permute-start.2) | collective-permute-done | bytes 786464 | tf_op jit(solution)/shard_map/ppermute | solution.py:204
  226.7 2.7 add_dynamic-update-slice_fusion
  229.4 0.0 collective-permute-done.3
  229.4 2.7 fusion
  232.1 2.4 convert_element_type.11
  234.5 0.3 pad_maximum_fusion.1
  234.8 16.0 %copy.27 = bf16[3,2048,256]{2,0,1:T(4,128)(2,1)S(1)} copy(bf16[3,2048,256]{2,1,0:T(8,128)(2,1)S(1)} %pad_maximum_fusion.1) | data formatting | bytes 6291456 | tf_op jit(solution)/shard_map/concatenate | solution.py:234
  250.8 52.6 %all_to_all.31 = bf16[3,2048,256]{2,0,1:T(4,128)(2,1)S(1)} all-to-all(bf16[3,2048,256]{2,0,1:T(4,128)(2,1)S(1)} %copy.27), channel_id=1, replica_groups=mesh['grp'=2,'blk'=4,'uly'=4] {'uly'}, dimensions={1} | all-to-all | bytes 6291456 | tf_op jit(solution)/shard_map/all_to_all | solution.py:235
  303.4 4.5 %fusion.2 = (bf16[1,512,4,256]{3,0,1,2:T(2,128)(2,1)S(1)}, bf16[1,512,4,256]{3,0,1,2:T(2,128)(2,1)S(1)}, bf16[1,512,4,256]{3,0,1,2:T(2,128)(2,1)S(1)}) fusion(bf16[3,512,4,256]{3,0,1,2:T(4,128)(2,1)S(1)} %bitcast.35), kind=kLoop, calls=%fused_computation.16 | loop fusion | bytes 6291456 | tf_op jit(solution)/shard_map/slice | solution.py:236
  307.9 1.4 copy.30
  309.2 1.2 copy.34
  310.4 1.4 copy.29
  311.8 1.2 copy.33
  313.0 1.4 copy.28
  314.3 1.2 copy.32
  (1 shorter events, 0.0 us)
Async XLA Ops:
  0.6 81.5 %copy-start = (s32[64,12]{0,1:T(8,128)S(1)}, s32[64,12]{0,1:T(8,128)}, u32[]{:S(2)}) copy-start(s32[64,12]{0,1:T(8,128)} %param.14) | copy-start | bytes 9220
  76.6 40.5 %copy-start.1 = (bf16[1,4,512,256]{3,2,1,0:T(8,128)(2,1)}, bf16[1,4,512,256]{3,2,1,0:T(8,128)(2,1)S(1)}, u32[]{:S(2)}) copy-start(bf16[1,4,512,256]{3,2,1,0:T(8,128)(2,1)S(1)} %get-tuple-element.38) | copy-start | bytes 3145732
  76.6 40.5 %copy-start.2 = (bf16[1,4,512,256]{3,2,1,0:T(8,128)(2,1)}, bf16[1,4,512,256]{3,2,1,0:T(8,128)(2,1)S(1)}, u32[]{:S(2)}) copy-start(bf16[1,4,512,256]{3,2,1,0:T(8,128)(2,1)S(1)} %get-tuple-element.39) | copy-start | bytes 3145732
  76.6 5.5 %copy-start.3 = (s32[64]{0:T(128)S(1)}, s32[64]{0:T(128)}, u32[]{:S(2)}) copy-start(s32[64]{0:T(128)} %param.15) | copy-start | bytes 772
  78.0 20.3 %collective-permute-start.1 = (bf16[2,768,256]{2,1,0:T(8,128)(2,1)}, bf16[2,768,256]{2,1,0:T(8,128)(2,1)}, u32[]{:S(2)}, u32[]{:S(2)}) collective-permute-start(bf16[2,768,256]{2,1,0:T(8,128)(2,1)} %get-tuple-element.42), channel_id=1, source_target_pairs={{4,0},{8,4},{12,8},{0,12},{5,1},{9,5},{13,9},{1,13},{6,2},{10,6},{... | collective-permute-start | bytes 2359304 | tf_op jit(solution)/shard_map/ppermute | solution.py:204
  82.1 33.9 %collective-permute-start = (bf16[2,768,256]{2,1,0:T(8,128)(2,1)}, bf16[2,768,256]{2,1,0:T(8,128)(2,1)}, u32[]{:S(2)}, u32[]{:S(2)}) collective-permute-start(bf16[2,768,256]{2,1,0:T(8,128)(2,1)} %get-tuple-element.43), channel_id=1, source_target_pairs={{12,0},{0,4},{4,8},{8,12},{13,1},{1,5},{5,9},{9,13},{14,2},{2,6},{... | collective-permute-start | bytes 2359304 | tf_op jit(solution)/shard_map/ppermute | solution.py:204
  192.7 34.0 %collective-permute-start.2 = (bf16[2,768,256]{2,1,0:T(8,128)(2,1)S(1)}, bf16[2,768,256]{2,1,0:T(8,128)(2,1)S(1)}, u32[]{:S(2)}, u32[]{:S(2)}) collective-permute-start(bf16[2,768,256]{2,1,0:T(8,128)(2,1)S(1)} %get-tuple-element.33), channel_id=1, source_target_pairs={{4,0},{8,4},{12,8},{0,12},{5,1},{9,5},{13,9},{1,13},{6,2},{10,6},{... | collective-permute-start | bytes 2359304 | tf_op jit(solution)/shard_map/ppermute | solution.py:204
  192.8 36.6 %collective-permute-start.3 = (bf16[2,768,256]{2,1,0:T(8,128)(2,1)S(1)}, bf16[2,768,256]{2,1,0:T(8,128)(2,1)S(1)}, u32[]{:S(2)}, u32[]{:S(2)}) collective-permute-start(bf16[2,768,256]{2,1,0:T(8,128)(2,1)S(1)} %get-tuple-element.34), channel_id=1, source_target_pairs={{12,0},{0,4},{4,8},{8,12},{13,1},{1,5},{5,9},{9,13},{14,2},{2,6},{... | collective-permute-start | bytes 2359304 | tf_op jit(solution)/shard_map/ppermute | solution.py:204
where the time goes:
time: 315 us; the launch traced here: 316 us
  blocking collectives  106 us (34%)
  Pallas kernels  75.5 us (24%)
  waiting for transfers between devices  64.9 us (21%)
  local copies, waits for them, and re-layouts  49.4 us (16%)
  other arithmetic  13.2 us (4%)
  starting transfers between devices  5.63 us (2%)
    pallas_call x1, Pallas kernels, attend(): pl.pallas_call(attend_kernel, grid_spec=pltpu.PrefetchScalarGridSpec(num_...  75.5 us
    ppermute x4, waiting for transfers between devices, passed_along(): lax.ppermute(block, axis, [((i - distance) % count, i) for i in range(cou...  64.9 us
    all_to_all x1, blocking collectives, shards(): lax.all_to_all(stacked, 'uly', split_axis=2, concat_axis=1, tiled=True)  53.5 us
    all_to_all x1, blocking collectives, shards(): lax.all_to_all(result, 'uly', split_axis=1, concat_axis=2, tiled=True)  52.6 us
    concatenate x1, local copies, waits for them, and re-layouts, shards(): result = jnp.concatenate([dq[None], own.astype(jnp.bfloat16)])  16 us
    slice x4, local copies, waits for them, and re-layouts, shards(): return (returned[0], returned[1], returned[2])  8.54 us
    another operation x1, local copies, waits for them, and re-layouts, shards(): stacked = jnp.stack([queries, keys, values, grad_out])  7.82 us
    all_to_all x1, local copies, waits for them, and re-layouts, shards(): lax.all_to_all(stacked, 'uly', split_axis=2, concat_axis=1, tiled=True)  7.43 us
  transfers between devices with their start and end apart: 4, of which 3 were waited for; matrix products, arithmetic and copies ran while one was open for 1% of the time, Pallas kernels for 0%

commit v1 on v0

--- a/solution.py
+++ b/solution.py
@@ -14,6 +14,7 @@
 SCALE = HD ** (-0.5)
 NT = (((1,), (1,)), ((), ()))
 MIB = 1024 * 1024
+MESH = pl.DeviceIdType.MESH
 
 
 def block_diagonal(pair, factor):
@@ -25,28 +26,23 @@
 
 
 def attend_kernel(
-    spots_ref, lengths_ref, q_ref, do_ref, kl_ref, ko_ref, kr_ref, vl_ref, vo_ref, vr_ref,
+    spots_ref, lengths_ref, q_ref, do_ref, k_ref, v_ref,
     dq_ref, own_ref, left_ref, right_ref,
     k_scr, v_scr, kt_scr, acc_k, acc_v, s_scr, p_scr, q_bd, do_bd, dqt_scr, round_scr, sems,
 ):
     step = pl.program_id(0)
     steps = pl.num_programs(0)
-    halo, feat = kl_ref.shape
-    rows = ko_ref.shape[0]
-    total = k_scr.shape[0]
+    halo = left_ref.shape[1]
+    total, feat = k_scr.shape
+    rows = total - 2 * halo
     packs = feat // PAIR
 
     @pl.when(step == 0)
     def _():
-        copies = []
-        for dst, parts in ((k_scr, (kl_ref, ko_ref, kr_ref)), (v_scr, (vl_ref, vo_ref, vr_ref))):
-            start = 0
-            for part in parts:
-                size = part.shape[0]
-                copies.append(
-                    pltpu.make_async_copy(part, dst.at[pl.ds(start, size)], sems.at[len(copies)])
-                )
-                start += size
+        copies = [
+            pltpu.make_async_copy(k_ref, k_scr, sems.at[0]),
+            pltpu.make_async_copy(v_ref, v_scr, sems.at[1]),
+        ]
         for copy in copies:
             copy.start()
 
@@ -157,10 +153,10 @@
             copy.wait()
 
 
-def attend(spots, lengths, q, do, k_parts, v_parts):
+def attend(spots, lengths, q, do, k, v):
     rows, feat = q.shape
-    halo = k_parts[0].shape[0]
-    total = rows + 2 * halo
+    total = k.shape[0]
+    halo = (total - rows) // 2
     packs = feat // PAIR
     slots = spots.shape[1]
     hbm = pl.BlockSpec(memory_space=pl.ANY)
@@ -171,7 +167,7 @@
         grid_spec=pltpu.PrefetchScalarGridSpec(
             num_scalar_prefetch=2,
             grid=(rows // BS,),
-            in_specs=[block, block] + [hbm] * 6,
+            in_specs=[block, block] + [hbm] * 2,
             out_specs=[block, hbm, hbm, hbm],
             scratch_shapes=[
                 pltpu.VMEM((total, feat), bf16),
@@ -196,12 +192,209 @@
         ],
         compiler_params=pltpu.CompilerParams(vmem_limit_bytes=48 * MIB),
         name="attend",
-    )(spots, lengths, q, do, *k_parts, *v_parts)
-
-
-def passed_along(block, axis, distance):
-    count = lax.axis_size(axis)
-    return lax.ppermute(block, axis, [((i - distance) % count, i) for i in range(count)])
+    )(spots, lengths, q, do, k, v)
+
+
+def greet(n):
+    me = lax.axis_index("uly")
+    count = lax.axis_size("blk")
+    rank = lax.axis_index("blk")
+    left, right = lax.rem(rank + count - 1, count), lax.rem(rank + 1, count)
+    barrier = pltpu.get_barrier_semaphore()
+    for d in range(1, n):
+        pl.semaphore_signal(barrier, 1, device_id={"uly": lax.rem(me + d, n)}, device_id_type=MESH)
+    for side in (left, right):
+        pl.semaphore_signal(barrier, 1, device_id={"blk": side}, device_id_type=MESH)
+    pl.semaphore_wait(barrier, n + 1)
+    return me, left, right
+
+
+def remote(src, dst, send, recv, where):
+    return pltpu.make_async_remote_copy(
+        src_ref=src, dst_ref=dst, send_sem=send, recv_sem=recv, device_id=where, device_id_type=MESH
+    )
+
+
+def distances(n):
+    return sorted(range(1, n), key=lambda d: -min(d, n - d))
+
+
+def spread_kernel(
+    n, q_ref, k_ref, v_ref, do_ref, q_out, do_out, k_out, v_out,
+    send_sem, recv_sem, own_sem, halo_send, halo_recv,
+):
+    me, left, right = greet(n)
+    part = q_ref.shape[0]
+    rows, feat = q_out.shape
+    halo = (k_out.shape[0] - rows) // 2
+    arrays = ((k_ref, k_out, halo), (v_ref, v_out, halo), (q_ref, q_out, 0), (do_ref, do_out, 0))
+    sent, kept = [], []
+    for a, (src, dst, offset) in enumerate(arrays):
+        here = dst.at[pl.ds(pl.multiple_of(offset + me * part, BS), part)]
+        mine = []
+        for d in distances(n):
+            peer = lax.rem(me + d, n)
+            copy = remote(
+                src.at[:, pl.ds(pl.multiple_of(peer * feat, feat), feat)], here,
+                send_sem.at[a, d], recv_sem.at[a, d], {"uly": peer},
+            )
+            copy.start()
+            mine.append(copy)
+        sent.append(mine)
+        copy = pltpu.make_async_copy(
+            src.at[:, pl.ds(pl.multiple_of(me * feat, feat), feat)], here, own_sem.at[a]
+        )
+        copy.start()
+        kept.append(copy)
+    halos = []
+    for a, out in enumerate((k_out, v_out)):
+        kept[a].wait()
+        for copy in sent[a]:
+            copy.wait_recv()
+        for i, (src, dst, side) in enumerate(((rows, 0, right), (halo, halo + rows, left))):
+            copy = remote(
+                out.at[pl.ds(src, halo)], out.at[pl.ds(dst, halo)],
+                halo_send.at[a, i], halo_recv.at[a, i], {"blk": side},
+            )
+            copy.start()
+            halos.append(copy)
+    for a in (2, 3):
+        kept[a].wait()
+        for copy in sent[a]:
+            copy.wait_recv()
+    for mine in sent:
+        for copy in mine:
+            copy.wait_send()
+    for copy in halos:
+        copy.wait()
+
+
+def spread(n, q, k, v, do):
+    part, width = q.shape
+    rows, feat = part * n, width // n
+    halo = REACHB * BS
+    hbm = pl.BlockSpec(memory_space=pl.ANY)
+    flat = jax.ShapeDtypeStruct((rows, feat), q.dtype)
+    near = jax.ShapeDtypeStruct((rows + 2 * halo, feat), q.dtype)
+    return pl.pallas_call(
+        functools.partial(spread_kernel, n),
+        in_specs=[hbm] * 4,
+        out_specs=[hbm] * 4,
+        out_shape=[flat, flat, near, near],
+        scratch_shapes=[
+            pltpu.SemaphoreType.DMA((4, n)),
+            pltpu.SemaphoreType.DMA((4, n)),
+            pltpu.SemaphoreType.DMA((4,)),
+            pltpu.SemaphoreType.DMA((2, 2)),
+            pltpu.SemaphoreType.DMA((2, 2)),
+        ],
+        compiler_params=pltpu.CompilerParams(collective_id=0, has_side_effects=True),
+        name="spread",
+    )(q, k, v, do)
+
+
+def collect_kernel(
+    n, dq_ref, own_ref, left_ref, right_ref, dq_out, dk_out, dv_out,
+    own_scr, res_scr, from_left, from_right,
+    send_sem, recv_sem, own_sem, load_sem, halo_send, halo_recv,
+):
+    me, left, right = greet(n)
+    _, rows, feat = own_ref.shape
+    halo = left_ref.shape[1]
+    part = rows // n
+    loads, halos = [], []
+    for a in range(2):
+        pair = (
+            remote(
+                left_ref.at[a], from_right.at[a],
+                halo_send.at[a, 0], halo_recv.at[a, 0], {"blk": left},
+            ),
+            remote(
+                right_ref.at[a], from_left.at[a],
+                halo_send.at[a, 1], halo_recv.at[a, 1], {"blk": right},
+            ),
+        )
+        for copy in pair:
+            copy.start()
+        halos.append(pair)
+        load = pltpu.make_async_copy(own_ref.at[a], own_scr.at[a], load_sem.at[a])
+        load.start()
+        loads.append(load)
+    pending, kept = [], []
+
+    def send(a, src, out):
+        there = out.at[:, pl.ds(pl.multiple_of(me * feat, feat), feat)]
+        for d in distances(n):
+            peer = lax.rem(me + d, n)
+            copy = remote(
+                src.at[pl.ds(pl.multiple_of(peer * part, part), part)], there,
+                send_sem.at[a, d], recv_sem.at[a, d], {"uly": peer},
+            )
+            copy.start()
+            pending.append(copy)
+        copy = pltpu.make_async_copy(
+            src.at[pl.ds(pl.multiple_of(me * part, part), part)], there, own_sem.at[a]
+        )
+        copy.start()
+        kept.append(copy)
+
+    send(2, dq_ref, dq_out)
+    for a in range(2):
+        loads[a].wait()
+
+        @pl.loop(halo // BS, (rows - halo) // BS)
+        def _(t):
+            at = pl.ds(pl.multiple_of(t * BS, BS), BS)
+            res_scr[a, at, :] = own_scr[a, at, :].astype(jnp.bfloat16)
+
+    for a, out in enumerate((dk_out, dv_out)):
+        for copy in halos[a]:
+            copy.wait_recv()
+
+        @pl.loop(0, halo // BS)
+        def _(t):
+            for base, arrived in ((0, from_left), (rows - halo, from_right)):
+                at = pl.ds(pl.multiple_of(base + t * BS, BS), BS)
+                more = arrived[a, pl.ds(pl.multiple_of(t * BS, BS), BS), :].astype(jnp.float32)
+                res_scr[a, at, :] = (own_scr[a, at, :] + more).astype(jnp.bfloat16)
+
+        send(a, res_scr.at[a], out)
+    for copy in kept:
+        copy.wait()
+    for copy in pending:
+        copy.wait()
+    for pair in halos:
+        for copy in pair:
+            copy.wait_send()
+
+
+def collect(n, dq, own, left, right):
+    rows, feat = dq.shape
+    halo = left.shape[1]
+    bf16 = jnp.bfloat16
+    hbm = pl.BlockSpec(memory_space=pl.ANY)
+    return pl.pallas_call(
+        functools.partial(collect_kernel, n),
+        in_specs=[hbm] * 4,
+        out_specs=[hbm] * 3,
+        out_shape=[jax.ShapeDtypeStruct((rows // n, feat * n), bf16)] * 3,
+        scratch_shapes=[
+            pltpu.VMEM((2, rows, feat), jnp.float32),
+            pltpu.VMEM((2, rows, feat), bf16),
+            pltpu.VMEM((2, halo, feat), bf16),
+            pltpu.VMEM((2, halo, feat), bf16),
+            pltpu.SemaphoreType.DMA((3, n)),
+            pltpu.SemaphoreType.DMA((3, n)),
+            pltpu.SemaphoreType.DMA((3,)),
+            pltpu.SemaphoreType.DMA((2,)),
+            pltpu.SemaphoreType.DMA((2, 2)),
+            pltpu.SemaphoreType.DMA((2, 2)),
+        ],
+        compiler_params=pltpu.CompilerParams(
+            collective_id=1, has_side_effects=True, vmem_limit_bytes=24 * MIB
+        ),
+        name="collect",
+    )(dq, own, left, right)
 
 
 def local_lists(key_lists, list_length, per_rank):
@@ -214,26 +407,11 @@
 
 
 def shards(queries, keys, values, grad_out, key_lists, list_length):
-    stacked = jnp.stack([queries, keys, values, grad_out])
-    spread = lax.all_to_all(stacked, "uly", split_axis=2, concat_axis=1, tiled=True)
-    q, k, v, do = spread[0], spread[1], spread[2], spread[3]
-    rows = q.shape[0]
-    halo = REACHB * BS
-    spots, lengths = local_lists(key_lists, list_length, rows // BS)
-    pair = jnp.stack([k, v])
-    from_left = passed_along(pair[:, rows - halo :], "blk", 1)
-    from_right = passed_along(pair[:, :halo], "blk", -1)
-    dq, own, left, right = attend(
-        spots, lengths, q, do,
-        (from_left[0], k, from_right[0]), (from_left[1], v, from_right[1]),
-    )
-    from_right = passed_along(left, "blk", -1).astype(jnp.float32)
-    from_left = passed_along(right, "blk", 1).astype(jnp.float32)
-    own = own.at[:, rows - halo :].add(from_right)
-    own = own.at[:, :halo].add(from_left)
-    result = jnp.concatenate([dq[None], own.astype(jnp.bfloat16)])
-    returned = lax.all_to_all(result, "uly", split_axis=1, concat_axis=2, tiled=True)
-    return (returned[0], returned[1], returned[2])
+    n = lax.axis_size("uly")
+    q, do, k, v = spread(n, queries, keys, values, grad_out)
+    spots, lengths = local_lists(key_lists, list_length, q.shape[0] // BS)
+    dq, own, left, right = attend(spots, lengths, q, do, k, v)
+    return tuple(collect(n, dq, own, left, right))
 
 
 def solution(mesh):

time: 315 us -> 182 us (0.58); the launches traced: 316 us -> 179 us
  blocking collectives: 106 us -> 0 us
  Pallas kernels: 75.5 us -> 170 us
  waiting for transfers between devices: 64.9 us -> 0 us
  local copies, waits for them, and re-layouts: 49.4 us -> 8.43 us
  other arithmetic: 13.2 us -> 0.01 us
  starting transfers between devices: 5.63 us -> 0 us
    pallas_call x0 -> x2, Pallas kernels: none -> 107 us  [the longest x1 54 us: collect(): pl.pallas_call(functools.partial(collect_kernel, n), in_specs=[hbm] * 4,...]
    all_to_all x2 -> x0, blocking collectives: 106 us -> none  [the longest x1 53.5 us: shards(): lax.all_to_all(stacked, 'uly', split_axis=2, concat_axis=1, tiled=True)]
    ppermute x4 -> x0, waiting for transfers between devices: 64.9 us -> none  [passed_along(): lax.ppermute(block, axis, [((i - distance) % count, i) for i in range(cou...]
    concatenate x1 -> x0, local copies, waits for them, and re-layouts: 16 us -> none  [shards(): result = jnp.concatenate([dq[None], own.astype(jnp.bfloat16)])]
    pallas_call x1, Pallas kernels: 75.5 us -> 63.4 us  [attend(): pl.pallas_call(attend_kernel, grid_spec=pltpu.PrefetchScalarGridSpec(num_...]
    slice x5 -> x0, local copies, waits for them, and re-layouts: 12 us -> none  [the longest x4 8.54 us: shards(): return (returned[0], returned[1], returned[2])]
    another operation x1 -> x0, local copies, waits for them, and re-layouts: 7.82 us -> none  [shards(): stacked = jnp.stack([queries, keys, values, grad_out])]
    all_to_all x1 -> x0, local copies, waits for them, and re-layouts: 7.43 us -> none  [shards(): lax.all_to_all(stacked, 'uly', split_axis=2, concat_axis=1, tiled=True)]
  transfers between devices with their start and end apart: 4 -> 0, of which waited for: 3 -> 0; matrix products, arithmetic and copies ran while one was open for 1% -> 0% of each run, Pallas kernels for 0% -> 0%
where the time goes in v1:
time: 182 us; the launch traced here: 179 us
  Pallas kernels  170 us (93%)
  local copies, waits for them, and re-layouts  8.43 us (5%)
    pallas_call x1, Pallas kernels, attend(): pl.pallas_call(attend_kernel, grid_spec=pltpu.PrefetchScalarGridSpec(num_...  63.4 us
    pallas_call x1, Pallas kernels, collect(): pl.pallas_call(functools.partial(collect_kernel, n), in_specs=[hbm] * 4,...  54 us
    pallas_call x1, Pallas kernels, spread(): pl.pallas_call(functools.partial(spread_kernel, n), in_specs=[hbm] * 4, o...  52.6 us
    unnamed x12, local copies, waits for them, and re-layouts  7.63 us

profile of v1, /device:TPU:1, one launch (start us, length us, event | category | flops | bytes accessed | tf_op | source)
XLA Modules:
  0.0 179.2 jit_solution(3668343122581605041)
XLA Ops:
  0.6 0.0 copy-start
  0.7 0.7 dynamic_slice.7.lengths_ref
  1.4 0.0 copy-done
  1.4 0.1 constant_dynamic-slice_fusion
  1.5 0.1 copy.10
  1.6 52.6 %spread.1 = (bf16[2048,256]{1,0:T(8,128)(2,1)}, bf16[2048,256]{1,0:T(8,128)(2,1)}, bf16[3584,256]{1,0:T(8,128)(2,1)}, bf16[3584,256]{1,0:T(8,128)(2,1)}) custom-call(bf16[512,1024]{1,0:T(8,128)(2,1)} %q_ref.1, bf16[512,1024]{1,0:T(8,128)(2,1)} %k_ref.1, bf16[512,1024]{1,0:T(8,128)(2,1)} %v_ref.1, bf16[512,1024]{1,0:T(8,128)(2,1)} %do_ref.1), custom_call_target="tpu_custom_call" | custom-call | tf_op jit(solution)/shard_map/spread/pallas_call | solution.py:279
  54.2 0.0 copy-start.2
  54.2 1.2 copy-done.2
  55.4 0.0 copy-start.3
  55.4 1.2 copy-done.3
  56.7 63.4 %attend.1 = (bf16[2048,256]{1,0:T(8,128)(2,1)S(1)}, f32[2,2048,256]{2,1,0:T(8,128)}, bf16[2,768,256]{2,1,0:T(8,128)(2,1)S(1)}, bf16[2,768,256]{2,1,0:T(8,128)(2,1)S(1)}) custom-call(s32[16,12]{1,0:T(8,128)S(1)} %add_select_fusion.spots_ref, s32[16]{0:T(128)S(1)} %dynamic_slice.7.lengths_ref, bf16[2048,256]{1,0:T(8,128)(2,1)S(1)} %copy-done.2, ...), custom_call_target="tpu_custom_call" | custom-call | tf_op jit(solution)/shard_map/attend/pallas_call | solution.py:165
  120.1 0.0 copy-start.1
  120.1 2.2 %copy-done.1 = f32[2,2048,256]{2,1,0:T(8,128)S(1)} copy-done((f32[2,2048,256]{2,1,0:T(8,128)S(1)}, f32[2,2048,256]{2,1,0:T(8,128)}, u32[]{:S(2)}) %copy-start.1) | copy-done | bytes 4194328
  122.3 54.0 %collect.1 = (bf16[512,1024]{1,0:T(8,128)(2,1)S(1)}, bf16[512,1024]{1,0:T(8,128)(2,1)S(1)}, bf16[512,1024]{1,0:T(8,128)(2,1)S(1)}) custom-call(bf16[2048,256]{1,0:T(8,128)(2,1)S(1)} %get-tuple-element.15.dq_ref, f32[2,2048,256]{2,1,0:T(8,128)S(1)} %copy-done.1, bf16[2,768,256]{2,1,0:T(8,128)(2,1)S(1)} %get-tuple-element.17.left_ref, ...), custom_call_target="tpu_custom_call" | custom-call | tf_op jit(solution)/shard_map/collect/pallas_call | solution.py:376
  176.3 1.0 copy.14
  177.2 1.0 copy.15
  178.2 1.0 copy.16
  (1 shorter events, 0.0 us)
Async XLA Ops:
  0.6 0.8 copy-start
  54.2 1.2 copy-start.2
  55.4 1.2 copy-start.3
  120.1 2.2 %copy-start.1 = (f32[2,2048,256]{2,1,0:T(8,128)S(1)}, f32[2,2048,256]{2,1,0:T(8,128)}, u32[]{:S(2)}) copy-start(f32[2,2048,256]{2,1,0:T(8,128)} %get-tuple-element.16.own_ref) | copy-start | bytes 12582916

commit v2 on v1

--- a/solution.py
+++ b/solution.py
@@ -12,7 +12,6 @@
 REACHB = 6
 PAIR = 2 * HD
 SCALE = HD ** (-0.5)
-NT = (((1,), (1,)), ((), ()))
 MIB = 1024 * 1024
 MESH = pl.DeviceIdType.MESH
 
@@ -28,7 +27,7 @@
 def attend_kernel(
     spots_ref, lengths_ref, q_ref, do_ref, k_ref, v_ref,
     dq_ref, own_ref, left_ref, right_ref,
-    k_scr, v_scr, kt_scr, acc_k, acc_v, s_scr, p_scr, q_bd, do_bd, dqt_scr, round_scr, sems,
+    k_scr, v_scr, kt_scr, acc_k, acc_v, s_scr, p_scr, g_scr, w_scr, q_bd, do_bd, q_bdt, do_bdt, dqt_scr, round_scr, sems,
 ):
     step = pl.program_id(0)
     steps = pl.num_programs(0)
@@ -67,21 +66,27 @@
         first, second = block_diagonal(do_ref[:, cols], 1.0)
         do_bd[g, :BS, :] = first
         do_bd[g, BS:, :] = second
+        q_bdt[g] = q_bd[g].T
+        do_bdt[g] = do_bd[g].T
 
     length = lengths_ref[step]
 
+    def block_of(slot):
+        return spots_ref[step, jnp.minimum(slot, length - 1)]
+
+    def products(slot):
+        at = pl.ds(pl.multiple_of(block_of(slot) * BS, BS), BS)
+        for g in range(packs):
+            cols = slice(g * PAIR, (g + 1) * PAIR)
+            s_scr[slot, g] = jnp.dot(k_scr[at, cols], q_bdt[g], preferred_element_type=jnp.float32)
+            p_scr[slot, g] = jnp.dot(v_scr[at, cols], do_bdt[g], preferred_element_type=jnp.float32)
+
     def scores(slot, carry):
-        at = pl.ds(pl.multiple_of(spots_ref[step, slot] * BS, BS), BS)
         out = []
         for g in range(packs):
             top, sums, cross = carry[g]
-            cols = slice(g * PAIR, (g + 1) * PAIR)
-            s = lax.dot_general(k_scr[at, cols], q_bd[g], NT, preferred_element_type=jnp.float32)
-            dp = lax.dot_general(v_scr[at, cols], do_bd[g], NT, preferred_element_type=jnp.float32)
-            s_scr[slot, g] = s
-            p_scr[slot, g] = dp
-            s = s.reshape(BS // 8, 8, 2 * BS)
-            dp = dp.reshape(BS // 8, 8, 2 * BS)
+            s = s_scr[slot, g].reshape(BS // 8, 8, 2 * BS)
+            dp = p_scr[slot, g].reshape(BS // 8, 8, 2 * BS)
             new_top = jnp.maximum(top, jnp.max(s, axis=0))
             keep = jnp.exp(top - new_top)
             p = jnp.exp(s - new_top[None])
@@ -92,8 +97,10 @@
                     cross * keep + jnp.sum(p * dp, axis=0),
                 )
             )
+        products(slot + 1)
         return tuple(out)
 
+    products(0)
     blank = jnp.zeros((8, 2 * BS), jnp.float32)
     start = tuple((blank - jnp.inf, blank, blank) for _ in range(packs))
     stats = lax.fori_loop(0, length, scores, start)
@@ -107,17 +114,20 @@
 
     dqt_scr[...] = jnp.zeros_like(dqt_scr)
 
-    @pl.loop(0, length)
-    def _(slot):
-        spot = spots_ref[step, slot]
+    def weights(slot):
+        for g in range(packs):
+            log_total, delta = merged[g]
+            weight = jnp.exp(s_scr[slot, g] - log_total)
+            g_scr[slot, g] = (weight * (p_scr[slot, g] - delta)).astype(jnp.bfloat16)
+            w_scr[slot, g] = weight.astype(jnp.bfloat16)
+
+    def sums(slot):
+        spot = block_of(slot)
         at = pl.ds(pl.multiple_of(spot * BS, BS), BS)
         for g in range(packs):
-            log_total, delta = merged[g]
             cols = slice(g * PAIR, (g + 1) * PAIR)
-            weight = jnp.exp(s_scr[slot, g] - log_total)
-            grad = (weight * (p_scr[slot, g] - delta)).astype(jnp.bfloat16)
-            half = weight.astype(jnp.bfloat16)
-            acc_v[at, cols] += jnp.dot(half, do_bd[g], preferred_element_type=jnp.float32)
+            grad = g_scr[slot, g]
+            acc_v[at, cols] += jnp.dot(w_scr[slot, g], do_bd[g], preferred_element_type=jnp.float32)
             acc_k[at, cols] += jnp.dot(grad, q_bd[g], preferred_element_type=jnp.float32)
             for h in range(2):
                 low = g * PAIR + h * HD
@@ -126,26 +136,34 @@
                     kt, grad[:, h * BS : (h + 1) * BS], preferred_element_type=jnp.float32
                 )
 
+    weights(0)
+
+    @pl.loop(1, length)
+    def _(slot):
+        sums(slot - 1)
+        weights(slot)
+
+    sums(length - 1)
+
     dq_ref[...] = (dqt_scr[...].T * SCALE).astype(jnp.bfloat16)
 
     @pl.when(step == steps - 1)
     def _():
-        @pl.loop(0, total // BS)
-        def _(b):
-            at = pl.ds(b * BS, BS)
-            round_scr[0, at, :] = acc_k[at, :].astype(jnp.bfloat16)
-            round_scr[1, at, :] = acc_v[at, :].astype(jnp.bfloat16)
+        for i, acc in enumerate((acc_k, acc_v)):
+            for side, base in enumerate((0, halo + rows)):
+
+                @pl.loop(0, halo // BS)
+                def _(b):
+                    round_scr[i, side, pl.ds(b * BS, BS), :] = acc[
+                        pl.ds(base + b * BS, BS), :
+                    ].astype(jnp.bfloat16)
 
         copies = []
         for i, acc in enumerate((acc_k, acc_v)):
             copies += [
                 pltpu.make_async_copy(acc.at[pl.ds(halo, rows)], own_ref.at[i], sems.at[3 * i]),
-                pltpu.make_async_copy(
-                    round_scr.at[i, pl.ds(0, halo)], left_ref.at[i], sems.at[3 * i + 1]
-                ),
-                pltpu.make_async_copy(
-                    round_scr.at[i, pl.ds(halo + rows, halo)], right_ref.at[i], sems.at[3 * i + 2]
-                ),
+                pltpu.make_async_copy(round_scr.at[i, 0], left_ref.at[i], sems.at[3 * i + 1]),
+                pltpu.make_async_copy(round_scr.at[i, 1], right_ref.at[i], sems.at[3 * i + 2]),
             ]
         for copy in copies:
             copy.start()
@@ -175,12 +193,16 @@
                 pltpu.VMEM((total // BS * feat, BS), bf16),
                 pltpu.VMEM((total, feat), f32),
                 pltpu.VMEM((total, feat), f32),
-                pltpu.VMEM((slots, packs, BS, 2 * BS), f32),
-                pltpu.VMEM((slots, packs, BS, 2 * BS), f32),
+                pltpu.VMEM((slots + 1, packs, BS, 2 * BS), f32),
+                pltpu.VMEM((slots + 1, packs, BS, 2 * BS), f32),
+                pltpu.VMEM((slots, packs, BS, 2 * BS), bf16),
+                pltpu.VMEM((slots, packs, BS, 2 * BS), bf16),
                 pltpu.VMEM((packs, 2 * BS, PAIR), bf16),
                 pltpu.VMEM((packs, 2 * BS, PAIR), bf16),
+                pltpu.VMEM((packs, PAIR, 2 * BS), bf16),
+                pltpu.VMEM((packs, PAIR, 2 * BS), bf16),
                 pltpu.VMEM((feat, BS), f32),
-                pltpu.VMEM((2, total, feat), bf16),
+                pltpu.VMEM((2, 2, halo, feat), bf16),
                 pltpu.SemaphoreType.DMA((6,)),
             ],
         ),
@@ -190,7 +212,7 @@
             jax.ShapeDtypeStruct((2, halo, feat), bf16),
             jax.ShapeDtypeStruct((2, halo, feat), bf16),
         ],
-        compiler_params=pltpu.CompilerParams(vmem_limit_bytes=48 * MIB),
+        compiler_params=pltpu.CompilerParams(vmem_limit_bytes=60 * MIB),
         name="attend",
     )(spots, lengths, q, do, k, v)
 
@@ -391,7 +413,7 @@
             pltpu.SemaphoreType.DMA((2, 2)),
         ],
         compiler_params=pltpu.CompilerParams(
-            collective_id=1, has_side_effects=True, vmem_limit_bytes=24 * MIB
+            collective_id=1, has_side_effects=True, vmem_limit_bytes=60 * MIB
         ),
         name="collect",
     )(dq, own, left, right)

time: 182 us -> 192 us (1.055); the launches traced: 179 us -> 194 us
  Pallas kernels: 170 us -> 187 us
  local copies, waits for them, and re-layouts: 8.43 us -> 5.79 us
    pallas_call x1, Pallas kernels: 54 us -> 64.1 us  [collect(): pl.pallas_call(functools.partial(collect_kernel, n), in_specs=[hbm] * 4,...]
    pallas_call x1, Pallas kernels: 63.4 us -> 70.7 us  [attend(): pl.pallas_call(attend_kernel, grid_spec=pltpu.PrefetchScalarGridSpec(num_...]
    unnamed x12 -> x10, local copies, waits for them, and re-layouts: 7.63 us -> 4.45 us
where the time goes in v2:
time: 192 us; the launch traced here: 194 us
  Pallas kernels  187 us (97%)
  local copies, waits for them, and re-layouts  5.79 us (3%)
    pallas_call x1, Pallas kernels, attend(): pl.pallas_call(attend_kernel, grid_spec=pltpu.PrefetchScalarGridSpec(num_...  70.7 us
    pallas_call x1, Pallas kernels, collect(): pl.pallas_call(functools.partial(collect_kernel, n), in_specs=[hbm] * 4,...  64.1 us
    pallas_call x1, Pallas kernels, spread(): pl.pallas_call(functools.partial(spread_kernel, n), in_specs=[hbm] * 4, o...  52.6 us
    unnamed x10, local copies, waits for them, and re-layouts  4.45 us

profile of v2, /device:TPU:1, one launch (start us, length us, event | category | flops | bytes accessed | tf_op | source)
XLA Modules:
  0.0 194.4 jit_solution(16294097473755104350)
XLA Ops:
  0.6 0.0 copy-start
  0.7 1.3 dynamic_slice.7.lengths_ref
  1.9 0.0 copy-done
  1.9 0.1 constant_dynamic-slice_fusion
  2.0 0.1 copy.10
  2.1 0.6 add_select_fusion.spots_ref
  2.7 52.6 %spread.1 = (bf16[2048,256]{1,0:T(8,128)(2,1)}, bf16[2048,256]{1,0:T(8,128)(2,1)}, bf16[3584,256]{1,0:T(8,128)(2,1)}, bf16[3584,256]{1,0:T(8,128)(2,1)}) custom-call(bf16[512,1024]{1,0:T(8,128)(2,1)} %q_ref.1, bf16[512,1024]{1,0:T(8,128)(2,1)} %k_ref.1, bf16[512,1024]{1,0:T(8,128)(2,1)} %v_ref.1, bf16[512,1024]{1,0:T(8,128)(2,1)} %do_ref.1), custom_call_target="tpu_custom_call" | custom-call | tf_op jit(solution)/shard_map/spread/pallas_call | solution.py:301
  55.3 70.7 %attend.1 = (bf16[2048,256]{1,0:T(8,128)(2,1)}, f32[2,2048,256]{2,1,0:T(8,128)}, bf16[2,768,256]{2,1,0:T(8,128)(2,1)}, bf16[2,768,256]{2,1,0:T(8,128)(2,1)}) custom-call(s32[16,12]{1,0:T(8,128)} %add_select_fusion.spots_ref, s32[16]{0:T(128)} %dynamic_slice.7.lengths_ref, bf16[2048,256]{1,0:T(8,128)(2,1)} %get-tuple-element.11.q_ref, ...), custom_call_target="tpu_custom_call" | custom-call | tf_op jit(solution)/shard_map/attend/pallas_call | solution.py:183
  125.9 64.1 %collect.1 = (bf16[512,1024]{1,0:T(8,128)(2,1)}, bf16[512,1024]{1,0:T(8,128)(2,1)}, bf16[512,1024]{1,0:T(8,128)(2,1)}) custom-call(bf16[2048,256]{1,0:T(8,128)(2,1)} %get-tuple-element.15.dq_ref, f32[2,2048,256]{2,1,0:T(8,128)} %get-tuple-element.16.own_ref, bf16[2,768,256]{2,1,0:T(8,128)(2,1)} %get-tuple-element.17.left_ref, ...), custom_call_target="tpu_custom_call" | custom-call | tf_op jit(solution)/shard_map/collect/pallas_call | solution.py:398
  190.1 0.0 copy-start.2
  190.1 0.0 copy-start.1
  190.1 2.4 %copy.14 = bf16[512,1024]{1,0:T(8,128)(2,1)} copy(bf16[512,1024]{1,0:T(8,128)(2,1)} %get-tuple-element.22) | data formatting | bytes 2097152
  192.5 0.0 copy-done.2
  192.5 1.0 copy.15
  193.5 0.0 copy-done.1
  193.5 1.0 copy.16
Async XLA Ops:
  0.6 1.3 copy-start
  190.1 2.4 %copy-start.2 = (bf16[512,1024]{1,0:T(8,128)(2,1)S(1)}, bf16[512,1024]{1,0:T(8,128)(2,1)}, u32[]{:S(2)}) copy-start(bf16[512,1024]{1,0:T(8,128)(2,1)} %get-tuple-element.23) | copy-start | bytes 3145732
  190.1 3.4 %copy-start.1 = (bf16[512,1024]{1,0:T(8,128)(2,1)S(1)}, bf16[512,1024]{1,0:T(8,128)(2,1)}, u32[]{:S(2)}) copy-start(bf16[512,1024]{1,0:T(8,128)(2,1)} %get-tuple-element.24) | copy-start | bytes 3145732

commit v3 on v2

--- a/solution.py
+++ b/solution.py
@@ -12,6 +12,7 @@
 REACHB = 6
 PAIR = 2 * HD
 SCALE = HD ** (-0.5)
+GROUPS = (4, 2, 1)
 MIB = 1024 * 1024
 MESH = pl.DeviceIdType.MESH
 
@@ -27,7 +28,7 @@
 def attend_kernel(
     spots_ref, lengths_ref, q_ref, do_ref, k_ref, v_ref,
     dq_ref, own_ref, left_ref, right_ref,
-    k_scr, v_scr, kt_scr, acc_k, acc_v, s_scr, p_scr, g_scr, w_scr, q_bd, do_bd, q_bdt, do_bdt, dqt_scr, round_scr, sems,
+    k_scr, v_scr, kt_scr, acc_k, acc_v, s_scr, p_scr, q_bd, do_bd, q_bdt, do_bdt, dqt_scr, round_scr, sems,
 ):
     step = pl.program_id(0)
     steps = pl.num_programs(0)
@@ -54,7 +55,7 @@
         for copy in copies:
             copy.wait()
 
-        @pl.loop(0, total // BS)
+        @pl.loop(0, total // BS, unroll=4)
         def _(b):
             kt_scr[pl.ds(b * feat, feat), :] = k_scr[pl.ds(b * BS, BS), :].T
 
@@ -70,23 +71,34 @@
         do_bdt[g] = do_bd[g].T
 
     length = lengths_ref[step]
-
-    def block_of(slot):
-        return spots_ref[step, jnp.minimum(slot, length - 1)]
-
-    def products(slot):
-        at = pl.ds(pl.multiple_of(block_of(slot) * BS, BS), BS)
-        for g in range(packs):
-            cols = slice(g * PAIR, (g + 1) * PAIR)
-            s_scr[slot, g] = jnp.dot(k_scr[at, cols], q_bdt[g], preferred_element_type=jnp.float32)
-            p_scr[slot, g] = jnp.dot(v_scr[at, cols], do_bdt[g], preferred_element_type=jnp.float32)
-
-    def scores(slot, carry):
+    groups, done = [], 0
+    for taken in GROUPS:
+        count = (length - done) // taken
+        groups.append((taken, done, count))
+        done = done + taken * count
+
+    def rows_of(slot, taken):
+        spots = [spots_ref[step, slot + i] for i in range(taken)]
+        return spots, [pl.ds(pl.multiple_of(spot * BS, BS), BS) for spot in spots]
+
+    def joined(pieces, axis=0):
+        return pieces[0] if len(pieces) == 1 else jnp.concatenate(pieces, axis=axis)
+
+    def scores(slot, carry, taken):
+        _, ats = rows_of(slot, taken)
         out = []
         for g in range(packs):
             top, sums, cross = carry[g]
-            s = s_scr[slot, g].reshape(BS // 8, 8, 2 * BS)
-            dp = p_scr[slot, g].reshape(BS // 8, 8, 2 * BS)
+            cols = slice(g * PAIR, (g + 1) * PAIR)
+            keys = joined([k_scr[at, cols] for at in ats])
+            values = joined([v_scr[at, cols] for at in ats])
+            s = jnp.dot(keys, q_bdt[g], preferred_element_type=jnp.float32)
+            dp = jnp.dot(values, do_bdt[g], preferred_element_type=jnp.float32)
+            for i in range(taken):
+                s_scr[slot + i, g] = s[i * BS : (i + 1) * BS]
+                p_scr[slot + i, g] = dp[i * BS : (i + 1) * BS]
+            s = s.reshape(taken * BS // 8, 8, 2 * BS)
+            dp = dp.reshape(taken * BS // 8, 8, 2 * BS)
             new_top = jnp.maximum(top, jnp.max(s, axis=0))
             keep = jnp.exp(top - new_top)
             p = jnp.exp(s - new_top[None])
@@ -97,13 +109,18 @@
                     cross * keep + jnp.sum(p * dp, axis=0),
                 )
             )
-        products(slot + 1)
         return tuple(out)
 
-    products(0)
     blank = jnp.zeros((8, 2 * BS), jnp.float32)
     start = tuple((blank - jnp.inf, blank, blank) for _ in range(packs))
-    stats = lax.fori_loop(0, length, scores, start)
+    stats = start
+    for taken, first, count in groups:
+        stats = lax.fori_loop(
+            0,
+            count,
+            lambda j, c, taken=taken, first=first: scores(first + taken * j, c, taken),
+            stats,
+        )
     merged = []
     for top, sums, cross in stats:
         best = jnp.max(top, axis=0, keepdims=True)
@@ -114,36 +131,36 @@
 
     dqt_scr[...] = jnp.zeros_like(dqt_scr)
 
-    def weights(slot):
+    def gradients(slot, taken):
+        spots, ats = rows_of(slot, taken)
         for g in range(packs):
             log_total, delta = merged[g]
-            weight = jnp.exp(s_scr[slot, g] - log_total)
-            g_scr[slot, g] = (weight * (p_scr[slot, g] - delta)).astype(jnp.bfloat16)
-            w_scr[slot, g] = weight.astype(jnp.bfloat16)
-
-    def sums(slot):
-        spot = block_of(slot)
-        at = pl.ds(pl.multiple_of(spot * BS, BS), BS)
-        for g in range(packs):
             cols = slice(g * PAIR, (g + 1) * PAIR)
-            grad = g_scr[slot, g]
-            acc_v[at, cols] += jnp.dot(w_scr[slot, g], do_bd[g], preferred_element_type=jnp.float32)
-            acc_k[at, cols] += jnp.dot(grad, q_bd[g], preferred_element_type=jnp.float32)
+            halves, grads = [], []
+            for i in range(taken):
+                weight = jnp.exp(s_scr[slot + i, g] - log_total)
+                grads.append((weight * (p_scr[slot + i, g] - delta)).astype(jnp.bfloat16))
+                halves.append(weight.astype(jnp.bfloat16))
+            grad, half = joined(grads), joined(halves)
+            dv = jnp.dot(half, do_bd[g], preferred_element_type=jnp.float32)
+            dk = jnp.dot(grad, q_bd[g], preferred_element_type=jnp.float32)
+            for i, at in enumerate(ats):
+                acc_v[at, cols] += dv[i * BS : (i + 1) * BS]
+                acc_k[at, cols] += dk[i * BS : (i + 1) * BS]
             for h in range(2):
                 low = g * PAIR + h * HD
-                kt = kt_scr[pl.ds(pl.multiple_of(spot * feat + low, HD), HD), :]
+                kt = joined(
+                    [kt_scr[pl.ds(pl.multiple_of(spot * feat + low, HD), HD), :] for spot in spots], 1
+                )
                 dqt_scr[low : low + HD, :] += jnp.dot(
                     kt, grad[:, h * BS : (h + 1) * BS], preferred_element_type=jnp.float32
                 )
 
-    weights(0)
-
-    @pl.loop(1, length)
-    def _(slot):
-        sums(slot - 1)
-        weights(slot)
-
-    sums(length - 1)
+    for taken, first, count in groups:
+
+        @pl.loop(0, count)
+        def _(j):
+            gradients(first + taken * j, taken)
 
     dq_ref[...] = (dqt_scr[...].T * SCALE).astype(jnp.bfloat16)
 
@@ -193,10 +210,8 @@
                 pltpu.VMEM((total // BS * feat, BS), bf16),
                 pltpu.VMEM((total, feat), f32),
                 pltpu.VMEM((total, feat), f32),
-                pltpu.VMEM((slots + 1, packs, BS, 2 * BS), f32),
-                pltpu.VMEM((slots + 1, packs, BS, 2 * BS), f32),
-                pltpu.VMEM((slots, packs, BS, 2 * BS), bf16),
-                pltpu.VMEM((slots, packs, BS, 2 * BS), bf16),
+                pltpu.VMEM((slots, packs, BS, 2 * BS), f32),
+                pltpu.VMEM((slots, packs, BS, 2 * BS), f32),
                 pltpu.VMEM((packs, 2 * BS, PAIR), bf16),
                 pltpu.VMEM((packs, 2 * BS, PAIR), bf16),
                 pltpu.VMEM((packs, PAIR, 2 * BS), bf16),

time: 192 us -> 163 us (0.85)
  Pallas kernels: 187 us -> 157 us
    pallas_call x1, Pallas kernels: 70.7 us -> 50.1 us  [attend(): pl.pallas_call(attend_kernel, grid_spec=pltpu.PrefetchScalarGridSpec(num_...]
    pallas_call x1, Pallas kernels: 64.1 us -> 54.1 us  [collect(): pl.pallas_call(functools.partial(collect_kernel, n), in_specs=[hbm] * 4,...]
where the time goes in v3:
time: 163 us; the launch traced here: 164 us
  Pallas kernels  157 us (96%)
  local copies, waits for them, and re-layouts  5.79 us (4%)
    pallas_call x1, Pallas kernels, collect(): pl.pallas_call(functools.partial(collect_kernel, n), in_specs=[hbm] * 4,...  54.1 us
    pallas_call x1, Pallas kernels, spread(): pl.pallas_call(functools.partial(spread_kernel, n), in_specs=[hbm] * 4, o...  52.6 us
    pallas_call x1, Pallas kernels, attend(): pl.pallas_call(attend_kernel, grid_spec=pltpu.PrefetchScalarGridSpec(num_...  50.1 us
    unnamed x10, local copies, waits for them, and re-layouts  4.45 us

profile of v3, /device:TPU:1, one launch (start us, length us, event | category | flops | bytes accessed | tf_op | source)
XLA Modules:
  0.0 163.8 jit_solution(3730788306888727893)
XLA Ops:
  0.6 0.0 copy-start
  0.7 1.3 dynamic_slice.7.lengths_ref
  1.9 0.0 copy-done
  1.9 0.1 constant_dynamic-slice_fusion
  2.0 0.1 copy.10
  2.1 0.6 add_select_fusion.spots_ref
  2.7 52.6 %spread.1 = (bf16[2048,256]{1,0:T(8,128)(2,1)}, bf16[2048,256]{1,0:T(8,128)(2,1)}, bf16[3584,256]{1,0:T(8,128)(2,1)}, bf16[3584,256]{1,0:T(8,128)(2,1)}) custom-call(bf16[512,1024]{1,0:T(8,128)(2,1)} %q_ref.1, bf16[512,1024]{1,0:T(8,128)(2,1)} %k_ref.1, bf16[512,1024]{1,0:T(8,128)(2,1)} %v_ref.1, bf16[512,1024]{1,0:T(8,128)(2,1)} %do_ref.1), custom_call_target="tpu_custom_call" | custom-call | tf_op jit(solution)/shard_map/spread/pallas_call | solution.py:316
  55.3 50.1 %attend.1 = (bf16[2048,256]{1,0:T(8,128)(2,1)}, f32[2,2048,256]{2,1,0:T(8,128)}, bf16[2,768,256]{2,1,0:T(8,128)(2,1)}, bf16[2,768,256]{2,1,0:T(8,128)(2,1)}) custom-call(s32[16,12]{1,0:T(8,128)} %add_select_fusion.spots_ref, s32[16]{0:T(128)} %dynamic_slice.7.lengths_ref, bf16[2048,256]{1,0:T(8,128)(2,1)} %get-tuple-element.11.q_ref, ...), custom_call_target="tpu_custom_call" | custom-call | tf_op jit(solution)/shard_map/attend/pallas_call | solution.py:200
  105.3 54.1 %collect.1 = (bf16[512,1024]{1,0:T(8,128)(2,1)}, bf16[512,1024]{1,0:T(8,128)(2,1)}, bf16[512,1024]{1,0:T(8,128)(2,1)}) custom-call(bf16[2048,256]{1,0:T(8,128)(2,1)} %get-tuple-element.15.dq_ref, f32[2,2048,256]{2,1,0:T(8,128)} %get-tuple-element.16.own_ref, bf16[2,768,256]{2,1,0:T(8,128)(2,1)} %get-tuple-element.17.left_ref, ...), custom_call_target="tpu_custom_call" | custom-call | tf_op jit(solution)/shard_map/collect/pallas_call | solution.py:413
  159.4 0.0 copy-start.2
  159.4 0.0 copy-start.1
  159.5 2.4 %copy.14 = bf16[512,1024]{1,0:T(8,128)(2,1)} copy(bf16[512,1024]{1,0:T(8,128)(2,1)} %get-tuple-element.22) | data formatting | bytes 2097152
  161.9 0.0 copy-done.2
  161.9 1.0 copy.15
  162.8 0.0 copy-done.1
  162.8 1.0 copy.16
Async XLA Ops:
  0.6 1.3 copy-start
  159.4 2.4 %copy-start.2 = (bf16[512,1024]{1,0:T(8,128)(2,1)S(1)}, bf16[512,1024]{1,0:T(8,128)(2,1)}, u32[]{:S(2)}) copy-start(bf16[512,1024]{1,0:T(8,128)(2,1)} %get-tuple-element.23) | copy-start | bytes 3145732
  159.4 3.4 %copy-start.1 = (bf16[512,1024]{1,0:T(8,128)(2,1)S(1)}, bf16[512,1024]{1,0:T(8,128)(2,1)}, u32[]{:S(2)}) copy-start(bf16[512,1024]{1,0:T(8,128)(2,1)} %get-tuple-element.24) | copy-start | bytes 3145732

commit v4 on v3

--- a/solution.py
+++ b/solution.py
@@ -256,6 +256,10 @@
     return sorted(range(1, n), key=lambda d: -min(d, n - d))
 
 
+def column_pieces(feat):
+    return [slice(start, start + PAIR) for start in range(0, feat, PAIR)]
+
+
 def spread_kernel(
     n, q_ref, k_ref, v_ref, do_ref, q_out, do_out, k_out, v_out,
     send_sem, recv_sem, own_sem, halo_send, halo_recv,
@@ -264,41 +268,45 @@
     part = q_ref.shape[0]
     rows, feat = q_out.shape
     halo = (k_out.shape[0] - rows) // 2
-    arrays = ((k_ref, k_out, halo), (v_ref, v_out, halo), (q_ref, q_out, 0), (do_ref, do_out, 0))
+    pieces = column_pieces(feat)
+    whole = slice(0, feat)
+    units = [(k_ref, k_out, halo, cols) for cols in pieces]
+    units += [(v_ref, v_out, halo, cols) for cols in pieces]
+    units += [(q_ref, q_out, 0, whole), (do_ref, do_out, 0, whole)]
+    near = 2 * len(pieces)
     sent, kept = [], []
-    for a, (src, dst, offset) in enumerate(arrays):
-        here = dst.at[pl.ds(pl.multiple_of(offset + me * part, BS), part)]
+    for u, (src, dst, offset, cols) in enumerate(units):
+        width = cols.stop - cols.start
+        here = dst.at[pl.ds(pl.multiple_of(offset + me * part, BS), part), cols]
         mine = []
         for d in distances(n):
             peer = lax.rem(me + d, n)
             copy = remote(
-                src.at[:, pl.ds(pl.multiple_of(peer * feat, feat), feat)], here,
-                send_sem.at[a, d], recv_sem.at[a, d], {"uly": peer},
+                src.at[:, pl.ds(pl.multiple_of(peer * feat + cols.start, PAIR), width)], here,
+                send_sem.at[u, d], recv_sem.at[u, d], {"uly": peer},
             )
             copy.start()
             mine.append(copy)
         sent.append(mine)
         copy = pltpu.make_async_copy(
-            src.at[:, pl.ds(pl.multiple_of(me * feat, feat), feat)], here, own_sem.at[a]
+            src.at[:, pl.ds(pl.multiple_of(me * feat + cols.start, PAIR), width)], here, own_sem.at[u]
         )
         copy.start()
         kept.append(copy)
     halos = []
-    for a, out in enumerate((k_out, v_out)):
-        kept[a].wait()
-        for copy in sent[a]:
+    for u, (_, out, _, cols) in enumerate(units):
+        kept[u].wait()
+        for copy in sent[u]:
             copy.wait_recv()
+        if u >= near:
+            continue
         for i, (src, dst, side) in enumerate(((rows, 0, right), (halo, halo + rows, left))):
             copy = remote(
-                out.at[pl.ds(src, halo)], out.at[pl.ds(dst, halo)],
-                halo_send.at[a, i], halo_recv.at[a, i], {"blk": side},
+                out.at[pl.ds(src, halo), cols], out.at[pl.ds(dst, halo), cols],
+                halo_send.at[u, i], halo_recv.at[u, i], {"blk": side},
             )
             copy.start()
             halos.append(copy)
-    for a in (2, 3):
-        kept[a].wait()
-        for copy in sent[a]:
-            copy.wait_recv()
     for mine in sent:
         for copy in mine:
             copy.wait_send()
@@ -312,18 +320,19 @@
     halo = REACHB * BS
     hbm = pl.BlockSpec(memory_space=pl.ANY)
     flat = jax.ShapeDtypeStruct((rows, feat), q.dtype)
-    near = jax.ShapeDtypeStruct((rows + 2 * halo, feat), q.dtype)
+    wide = jax.ShapeDtypeStruct((rows + 2 * halo, feat), q.dtype)
+    near = 2 * len(column_pieces(feat))
     return pl.pallas_call(
         functools.partial(spread_kernel, n),
         in_specs=[hbm] * 4,
         out_specs=[hbm] * 4,
-        out_shape=[flat, flat, near, near],
+        out_shape=[flat, flat, wide, wide],
         scratch_shapes=[
-            pltpu.SemaphoreType.DMA((4, n)),
-            pltpu.SemaphoreType.DMA((4, n)),
-            pltpu.SemaphoreType.DMA((4,)),
-            pltpu.SemaphoreType.DMA((2, 2)),
-            pltpu.SemaphoreType.DMA((2, 2)),
+            pltpu.SemaphoreType.DMA((near + 2, n)),
+            pltpu.SemaphoreType.DMA((near + 2, n)),
+            pltpu.SemaphoreType.DMA((near + 2,)),
+            pltpu.SemaphoreType.DMA((near, 2)),
+            pltpu.SemaphoreType.DMA((near, 2)),
         ],
         compiler_params=pltpu.CompilerParams(collective_id=0, has_side_effects=True),
         name="spread",
@@ -339,43 +348,44 @@
     _, rows, feat = own_ref.shape
     halo = left_ref.shape[1]
     part = rows // n
-    loads, halos = [], []
-    for a in range(2):
+    units = [(a, cols) for a in range(2) for cols in column_pieces(feat)]
+    halos = []
+    for u, (a, cols) in enumerate(units):
         pair = (
             remote(
-                left_ref.at[a], from_right.at[a],
-                halo_send.at[a, 0], halo_recv.at[a, 0], {"blk": left},
+                left_ref.at[a, :, cols], from_right.at[a, :, cols],
+                halo_send.at[u, 0], halo_recv.at[u, 0], {"blk": left},
             ),
             remote(
-                right_ref.at[a], from_left.at[a],
-                halo_send.at[a, 1], halo_recv.at[a, 1], {"blk": right},
+                right_ref.at[a, :, cols], from_left.at[a, :, cols],
+                halo_send.at[u, 1], halo_recv.at[u, 1], {"blk": right},
             ),
         )
         for copy in pair:
             copy.start()
         halos.append(pair)
-        load = pltpu.make_async_copy(own_ref.at[a], own_scr.at[a], load_sem.at[a])
+    loads = [pltpu.make_async_copy(own_ref.at[a], own_scr.at[a], load_sem.at[a]) for a in range(2)]
+    for load in loads:
         load.start()
-        loads.append(load)
     pending, kept = [], []
 
-    def send(a, src, out):
-        there = out.at[:, pl.ds(pl.multiple_of(me * feat, feat), feat)]
+    def send(u, rows_from, out, start, width):
+        there = out.at[:, pl.ds(pl.multiple_of(me * feat + start, PAIR), width)]
         for d in distances(n):
             peer = lax.rem(me + d, n)
             copy = remote(
-                src.at[pl.ds(pl.multiple_of(peer * part, part), part)], there,
-                send_sem.at[a, d], recv_sem.at[a, d], {"uly": peer},
+                rows_from(pl.ds(pl.multiple_of(peer * part, BS), part)), there,
+                send_sem.at[u, d], recv_sem.at[u, d], {"uly": peer},
             )
             copy.start()
             pending.append(copy)
         copy = pltpu.make_async_copy(
-            src.at[pl.ds(pl.multiple_of(me * part, part), part)], there, own_sem.at[a]
+            rows_from(pl.ds(pl.multiple_of(me * part, BS), part)), there, own_sem.at[u]
         )
         copy.start()
         kept.append(copy)
 
-    send(2, dq_ref, dq_out)
+    send(len(units), lambda at: dq_ref.at[at], dq_out, 0, feat)
     for a in range(2):
         loads[a].wait()
 
@@ -384,18 +394,21 @@
             at = pl.ds(pl.multiple_of(t * BS, BS), BS)
             res_scr[a, at, :] = own_scr[a, at, :].astype(jnp.bfloat16)
 
-    for a, out in enumerate((dk_out, dv_out)):
-        for copy in halos[a]:
+    for u, (a, cols) in enumerate(units):
+        for copy in halos[u]:
             copy.wait_recv()
 
         @pl.loop(0, halo // BS)
         def _(t):
             for base, arrived in ((0, from_left), (rows - halo, from_right)):
                 at = pl.ds(pl.multiple_of(base + t * BS, BS), BS)
-                more = arrived[a, pl.ds(pl.multiple_of(t * BS, BS), BS), :].astype(jnp.float32)
-                res_scr[a, at, :] = (own_scr[a, at, :] + more).astype(jnp.bfloat16)
-
-        send(a, res_scr.at[a], out)
+                more = arrived[a, pl.ds(pl.multiple_of(t * BS, BS), BS), cols].astype(jnp.float32)
+                res_scr[a, at, cols] = (own_scr[a, at, cols] + more).astype(jnp.bfloat16)
+
+        send(
+            u, lambda at: res_scr.at[a, at, cols], (dk_out, dv_out)[a],
+            cols.start, cols.stop - cols.start,
+        )
     for copy in kept:
         copy.wait()
     for copy in pending:
@@ -408,6 +421,7 @@
 def collect(n, dq, own, left, right):
     rows, feat = dq.shape
     halo = left.shape[1]
+    near = 2 * len(column_pieces(feat))
     bf16 = jnp.bfloat16
     hbm = pl.BlockSpec(memory_space=pl.ANY)
     return pl.pallas_call(
@@ -420,12 +434,12 @@
             pltpu.VMEM((2, rows, feat), bf16),
             pltpu.VMEM((2, halo, feat), bf16),
             pltpu.VMEM((2, halo, feat), bf16),
-            pltpu.SemaphoreType.DMA((3, n)),
-            pltpu.SemaphoreType.DMA((3, n)),
-            pltpu.SemaphoreType.DMA((3,)),
+            pltpu.SemaphoreType.DMA((near + 1, n)),
+            pltpu.SemaphoreType.DMA((near + 1, n)),
+            pltpu.SemaphoreType.DMA((near + 1,)),
             pltpu.SemaphoreType.DMA((2,)),
-            pltpu.SemaphoreType.DMA((2, 2)),
-            pltpu.SemaphoreType.DMA((2, 2)),
+            pltpu.SemaphoreType.DMA((near, 2)),
+            pltpu.SemaphoreType.DMA((near, 2)),
         ],
         compiler_params=pltpu.CompilerParams(
             collective_id=1, has_side_effects=True, vmem_limit_bytes=60 * MIB

time: 163 us -> 158 us (0.969)
  the two profiles are of different devices: /device:TPU:1 before, /device:TPU:7 now
where the time goes in v4:
time: 158 us; the launch traced here: 156 us
  Pallas kernels  149 us (94%)
  local copies, waits for them, and re-layouts  5.79 us (4%)
    pallas_call x1, Pallas kernels, spread(): pl.pallas_call(functools.partial(spread_kernel, n), in_specs=[hbm] * 4, o...  50.5 us
    pallas_call x1, Pallas kernels, collect(): pl.pallas_call(functools.partial(collect_kernel, n), in_specs=[hbm] * 4,...  50.3 us
    pallas_call x1, Pallas kernels, attend(): pl.pallas_call(attend_kernel, grid_spec=pltpu.PrefetchScalarGridSpec(num_...  48.6 us
    unnamed x10, local copies, waits for them, and re-layouts  4.45 us

profile of v4, /device:TPU:7, one launch (start us, length us, event | category | flops | bytes accessed | tf_op | source)
XLA Modules:
  0.0 156.4 jit_solution(16311518361367634946)
XLA Ops:
  0.6 0.0 copy-start
  0.7 1.3 dynamic_slice.7.lengths_ref
  1.9 0.0 copy-done
  1.9 0.1 constant_dynamic-slice_fusion
  2.0 0.1 copy.10
  2.1 0.6 add_select_fusion.spots_ref
  2.7 50.5 %spread.1 = (bf16[2048,256]{1,0:T(8,128)(2,1)}, bf16[2048,256]{1,0:T(8,128)(2,1)}, bf16[3584,256]{1,0:T(8,128)(2,1)}, bf16[3584,256]{1,0:T(8,128)(2,1)}) custom-call(bf16[512,1024]{1,0:T(8,128)(2,1)} %q_ref.1, bf16[512,1024]{1,0:T(8,128)(2,1)} %k_ref.1, bf16[512,1024]{1,0:T(8,128)(2,1)} %v_ref.1, bf16[512,1024]{1,0:T(8,128)(2,1)} %do_ref.1), custom_call_target="tpu_custom_call" | custom-call | tf_op jit(solution)/shard_map/spread/pallas_call | solution.py:325
  53.2 48.6 %attend.1 = (bf16[2048,256]{1,0:T(8,128)(2,1)}, f32[2,2048,256]{2,1,0:T(8,128)}, bf16[2,768,256]{2,1,0:T(8,128)(2,1)}, bf16[2,768,256]{2,1,0:T(8,128)(2,1)}) custom-call(s32[16,12]{1,0:T(8,128)} %add_select_fusion.spots_ref, s32[16]{0:T(128)} %dynamic_slice.7.lengths_ref, bf16[2048,256]{1,0:T(8,128)(2,1)} %get-tuple-element.11.q_ref, ...), custom_call_target="tpu_custom_call" | custom-call | tf_op jit(solution)/shard_map/attend/pallas_call | solution.py:200
  101.7 50.3 %collect.1 = (bf16[512,1024]{1,0:T(8,128)(2,1)}, bf16[512,1024]{1,0:T(8,128)(2,1)}, bf16[512,1024]{1,0:T(8,128)(2,1)}) custom-call(bf16[2048,256]{1,0:T(8,128)(2,1)} %get-tuple-element.15.dq_ref, f32[2,2048,256]{2,1,0:T(8,128)} %get-tuple-element.16.own_ref, bf16[2,768,256]{2,1,0:T(8,128)(2,1)} %get-tuple-element.17.left_ref, ...), custom_call_target="tpu_custom_call" | custom-call | tf_op jit(solution)/shard_map/collect/pallas_call | solution.py:427
  152.0 0.0 copy-start.2
  152.1 0.0 copy-start.1
  152.1 2.4 %copy.14 = bf16[512,1024]{1,0:T(8,128)(2,1)} copy(bf16[512,1024]{1,0:T(8,128)(2,1)} %get-tuple-element.22) | data formatting | bytes 2097152
  154.5 0.0 copy-done.2
  154.5 1.0 copy.15
  155.5 0.0 copy-done.1
  155.5 1.0 copy.16
Async XLA Ops:
  0.6 1.3 copy-start
  152.0 2.4 %copy-start.2 = (bf16[512,1024]{1,0:T(8,128)(2,1)S(1)}, bf16[512,1024]{1,0:T(8,128)(2,1)}, u32[]{:S(2)}) copy-start(bf16[512,1024]{1,0:T(8,128)(2,1)} %get-tuple-element.23) | copy-start | bytes 3145732
  152.1 3.4 %copy-start.1 = (bf16[512,1024]{1,0:T(8,128)(2,1)S(1)}, bf16[512,1024]{1,0:T(8,128)(2,1)}, u32[]{:S(2)}) copy-start(bf16[512,1024]{1,0:T(8,128)(2,1)} %get-tuple-element.24) | copy-start | bytes 3145732

commit v5 on v4

--- a/solution.py
+++ b/solution.py
@@ -52,12 +52,13 @@
             acc_k[at, :] = jnp.zeros((BS, feat), jnp.float32)
             acc_v[at, :] = jnp.zeros((BS, feat), jnp.float32)
 
-        for copy in copies:
-            copy.wait()
+        copies[0].wait()
 
         @pl.loop(0, total // BS, unroll=4)
         def _(b):
             kt_scr[pl.ds(b * feat, feat), :] = k_scr[pl.ds(b * BS, BS), :].T
+
+        copies[1].wait()
 
     for g in range(packs):
         cols = slice(g * PAIR, (g + 1) * PAIR)
@@ -166,24 +167,25 @@
 
     @pl.when(step == steps - 1)
     def _():
+        copies = []
+
+        def begin(src, dst):
+            copy = pltpu.make_async_copy(src, dst, sems.at[len(copies)])
+            copy.start()
+            copies.append(copy)
+
         for i, acc in enumerate((acc_k, acc_v)):
-            for side, base in enumerate((0, halo + rows)):
-
-                @pl.loop(0, halo // BS)
+            begin(acc.at[pl.ds(halo, rows)], own_ref.at[i])
+        for i, acc in enumerate((acc_k, acc_v)):
+            for side, (base, out) in enumerate(((0, left_ref), (halo + rows, right_ref))):
+
+                @pl.loop(0, halo // BS, unroll=2)
                 def _(b):
                     round_scr[i, side, pl.ds(b * BS, BS), :] = acc[
                         pl.ds(base + b * BS, BS), :
                     ].astype(jnp.bfloat16)
 
-        copies = []
-        for i, acc in enumerate((acc_k, acc_v)):
-            copies += [
-                pltpu.make_async_copy(acc.at[pl.ds(halo, rows)], own_ref.at[i], sems.at[3 * i]),
-                pltpu.make_async_copy(round_scr.at[i, 0], left_ref.at[i], sems.at[3 * i + 1]),
-                pltpu.make_async_copy(round_scr.at[i, 1], right_ref.at[i], sems.at[3 * i + 2]),
-            ]
-        for copy in copies:
-            copy.start()
+                begin(round_scr.at[i, side], out.at[i])
         for copy in copies:
             copy.wait()
 

time: 158 us -> 156 us (0.987)
  the two profiles are of different devices: /device:TPU:7 before, /device:TPU:1 now
where the time goes in v5:
time: 156 us; the launch traced here: 154 us
  Pallas kernels  147 us (94%)
  local copies, waits for them, and re-layouts  5.79 us (4%)
    pallas_call x1, Pallas kernels, spread(): pl.pallas_call(functools.partial(spread_kernel, n), in_specs=[hbm] * 4, o...  52.2 us
    pallas_call x1, Pallas kernels, collect(): pl.pallas_call(functools.partial(collect_kernel, n), in_specs=[hbm] * 4,...  49.8 us
    pallas_call x1, Pallas kernels, attend(): pl.pallas_call(attend_kernel, grid_spec=pltpu.PrefetchScalarGridSpec(num_...  45.2 us
    unnamed x10, local copies, waits for them, and re-layouts  4.45 us

profile of v5, /device:TPU:1, one launch (start us, length us, event | category | flops | bytes accessed | tf_op | source)
XLA Modules:
  0.0 154.3 jit_solution(12920997013501615095)
XLA Ops:
  0.6 0.0 copy-start
  0.7 1.3 dynamic_slice.7.lengths_ref
  1.9 0.0 copy-done
  1.9 0.1 constant_dynamic-slice_fusion
  2.0 0.1 copy.10
  2.1 0.6 add_select_fusion.spots_ref
  2.7 52.2 %spread.1 = (bf16[2048,256]{1,0:T(8,128)(2,1)}, bf16[2048,256]{1,0:T(8,128)(2,1)}, bf16[3584,256]{1,0:T(8,128)(2,1)}, bf16[3584,256]{1,0:T(8,128)(2,1)}) custom-call(bf16[512,1024]{1,0:T(8,128)(2,1)} %q_ref.1, bf16[512,1024]{1,0:T(8,128)(2,1)} %k_ref.1, bf16[512,1024]{1,0:T(8,128)(2,1)} %v_ref.1, bf16[512,1024]{1,0:T(8,128)(2,1)} %do_ref.1), custom_call_target="tpu_custom_call" | custom-call | tf_op jit(solution)/shard_map/spread/pallas_call | solution.py:327
  54.9 45.2 %attend.1 = (bf16[2048,256]{1,0:T(8,128)(2,1)}, f32[2,2048,256]{2,1,0:T(8,128)}, bf16[2,768,256]{2,1,0:T(8,128)(2,1)}, bf16[2,768,256]{2,1,0:T(8,128)(2,1)}) custom-call(s32[16,12]{1,0:T(8,128)} %add_select_fusion.spots_ref, s32[16]{0:T(128)} %dynamic_slice.7.lengths_ref, bf16[2048,256]{1,0:T(8,128)(2,1)} %get-tuple-element.11.q_ref, ...), custom_call_target="tpu_custom_call" | custom-call | tf_op jit(solution)/shard_map/attend/pallas_call | solution.py:202
  100.1 49.8 %collect.1 = (bf16[512,1024]{1,0:T(8,128)(2,1)}, bf16[512,1024]{1,0:T(8,128)(2,1)}, bf16[512,1024]{1,0:T(8,128)(2,1)}) custom-call(bf16[2048,256]{1,0:T(8,128)(2,1)} %get-tuple-element.15.dq_ref, f32[2,2048,256]{2,1,0:T(8,128)} %get-tuple-element.16.own_ref, bf16[2,768,256]{2,1,0:T(8,128)(2,1)} %get-tuple-element.17.left_ref, ...), custom_call_target="tpu_custom_call" | custom-call | tf_op jit(solution)/shard_map/collect/pallas_call | solution.py:429
  150.0 0.0 copy-start.2
  150.0 0.0 copy-start.1
  150.0 2.4 %copy.14 = bf16[512,1024]{1,0:T(8,128)(2,1)} copy(bf16[512,1024]{1,0:T(8,128)(2,1)} %get-tuple-element.22) | data formatting | bytes 2097152
  152.4 0.0 copy-done.2
  152.4 1.0 copy.15
  153.4 0.0 copy-done.1
  153.4 1.0 copy.16
Async XLA Ops:
  0.6 1.3 copy-start
  150.0 2.4 %copy-start.2 = (bf16[512,1024]{1,0:T(8,128)(2,1)S(1)}, bf16[512,1024]{1,0:T(8,128)(2,1)}, u32[]{:S(2)}) copy-start(bf16[512,1024]{1,0:T(8,128)(2,1)} %get-tuple-element.23) | copy-start | bytes 3145732
  150.0 3.4 %copy-start.1 = (bf16[512,1024]{1,0:T(8,128)(2,1)S(1)}, bf16[512,1024]{1,0:T(8,128)(2,1)}, u32[]{:S(2)}) copy-start(bf16[512,1024]{1,0:T(8,128)(2,1)} %get-tuple-element.24) | copy-start | bytes 3145732
